TPU v7x, 256 devices: a whole 4x4x8 slice. The times are simulated.
256 devices in a mesh: section: 8 (over z_lo, y), fsdp: 32 (over z_hi, x, core).
Axes of the slice: x: 4, y: 4, z: 8 (z_hi: 4, z_lo: 2; z = z_hi * 2 + z_lo), core: 2. Of those that a mesh axis runs over, the one named last changes fastest.
Arguments:
- hidden: bfloat16 [16384, 7168], P('fsdp', 'section'), may hold values from -600 to 600
- token_ids: int32 [16384], P('fsdp'), may hold values from 0 to 65535
- table: bfloat16 [7168, 65536], P(('section', 'fsdp')), may hold values from -600 to 600
- gain_hidden: float32 [7168], replicated, may hold values from 0.1 to 1.9
- gain_embed: float32 [7168], replicated, may hold values from 0.1 to 1.9
- proj_hidden: bfloat16 [7168, 4096], P(('section', 'fsdp')), may hold values from -0.046875 to 0.046875
- proj_embed: bfloat16 [7168, 4096], P(('section', 'fsdp')), may hold values from -0.046875 to 0.046875
Outputs:
- mixed: bfloat16 [16384, 4096], P('fsdp', 'section')
All inputs are finite; a program needn't handle non-finite values.
Results may differ from a plain program's by a relative error of at most 0.0049.
Values may be sent and summed in bfloat16 or wider, within the bound.
No kernel may reach another device: no remote copies, remote signals or barrier semaphores. Data moves between devices by JAX's collectives and lax.ppermute only.
A program may use at most 128 MiB of HBM per device.

v0:
```python
import jax
import jax.numpy as jnp
from jax import lax
from jax.sharding import PartitionSpec as P

EPS = 1e-06


def on_device(hidden, token_ids, table, gain_hidden, gain_embed, proj_hidden, proj_embed):
    model_width = gain_hidden.shape[0]
    block_width = hidden.shape[1]
    tokens_here = hidden.shape[0]
    shard_rows = proj_hidden.shape[0]
    sections = lax.axis_size("section")
    groups = lax.axis_size("fsdp")
    section_pos = lax.axis_index("section")
    every_id = lax.all_gather(token_ids, "fsdp", axis=0, tiled=True)
    shifted = jnp.roll(every_id, -1)
    looked = jnp.take(table, shifted, axis=1)
    embed_block = lax.all_to_all(looked, "fsdp", split_axis=1, concat_axis=0, tiled=True)
    hidden_f = hidden.astype(jnp.float32)
    embed_f = embed_block.astype(jnp.float32)
    hidden_sq, embed_sq = lax.psum(
        (jnp.sum(hidden_f * hidden_f, axis=1), jnp.sum(embed_f * embed_f, axis=0)), "section"
    )
    hidden_scale = lax.rsqrt(hidden_sq / model_width + EPS)
    embed_scale = lax.rsqrt(embed_sq / model_width + EPS)
    gain_h = lax.dynamic_slice_in_dim(gain_hidden, section_pos * block_width, block_width)
    gain_e = lax.dynamic_slice_in_dim(gain_embed, section_pos * block_width, block_width)
    hidden_norm = (hidden_f * hidden_scale[:, None] * gain_h[None, :]).astype(jnp.bfloat16)
    embed_norm = (embed_f * embed_scale[None, :] * gain_e[:, None]).astype(jnp.bfloat16)
    hidden_panel, embed_panel = (
        lax.all_to_all(proj_hidden, "section", split_axis=1, concat_axis=0, tiled=True),
        lax.all_to_all(proj_embed, "section", split_axis=1, concat_axis=0, tiled=True),
    )
    hidden_all, embed_all = (
        lax.all_gather(hidden_norm, "section", axis=1, tiled=True),
        lax.all_gather(embed_norm, "section", axis=0, tiled=True),
    )
    hidden_split = hidden_all.reshape(tokens_here, sections, groups, shard_rows)
    embed_split = embed_all.reshape(sections, groups, shard_rows, tokens_here)
    pieces = (
        lax.all_gather(hidden_panel, "fsdp", axis=0, tiled=True),
        lax.all_gather(embed_panel, "fsdp", axis=0, tiled=True),
    )
    count = pieces[0].shape[0]
    left = hidden_split
    left = left.transpose(0, 2, 1, 3).reshape(tokens_here, count)
    right = embed_split
    right = right.transpose(1, 0, 2, 3).reshape(count, tokens_here)
    left, right = (left, right)
    total = jnp.dot(left, pieces[0], preferred_element_type=jnp.float32)
    mixed = total + lax.dot_general(
        right, pieces[1], (((0,), (0,)), ((), ())), preferred_element_type=jnp.float32
    )
    return mixed.astype(jnp.bfloat16)


def solution(mesh):
    placed = (
        P("fsdp", "section"),
        P("fsdp"),
        P(("section", "fsdp"), None),
        P(),
        P(),
        P(("section", "fsdp"), None),
        P(("section", "fsdp"), None),
    )
    return jax.shard_map(
        on_device, mesh=mesh, in_specs=placed, out_specs=P("fsdp", "section"), check_vma=False
    )
```

profile of v0, /device:TPU:1, one launch (start us, length us, event | category | flops | bytes accessed | tf_op | source)
XLA Modules:
  0.0 526.5 jit_solution(9763572431352885462)
XLA Ops:
  6.5 49.0 %all-gather = s32[32,1,512]{2,1,0:T(1,128)S(1)} all-gather(s32[1,1,512]{2,1,0:T(1,128)} %bitcast.41), channel_id=1, replica_groups=mesh['section'=8,'fsdp'=32] {'fsdp'}, dimensions={0}, use_global_device_ids=true | all-gather | bytes 67584 | tf_op jit(solution)/shard_map/all_gather | solution.py:17
  55.5 0.5 slice.13
  56.1 0.1 slice.12
  56.1 13.9 %copy.19 = bf16[28,65536]{0,1:T(8,128)(2,1)} copy(bf16[28,65536]{1,0:T(8,128)(2,1)} %param.9) | data formatting | bytes 7340032 | tf_op args[2]
  70.1 0.7 pad_add_fusion
  70.8 0.8 compare_select_fusion
  71.6 0.0 copy-start
  71.6 63.3 %gather_fusion = bf16[16384,28]{1,0:T(8,128)(2,1)} fusion(bf16[28,65536]{0,1:T(8,128)(2,1)} %copy.19, s32[16384]{0:T(1024)S(1)} %broadcast_clamp_fusion), kind=kCustom, calls=%fused_computation | custom fusion | bytes 1900544 | tf_op jit(solution)/shard_map/jit(_take)/gather | solution.py:19
  134.9 3.7 copy.20
  138.7 1.1 broadcast_select_fusion
  139.8 3.8 all-to-all-start.1
  143.6 0.0 all-gather.6.cloned.1.call-start
  143.6 0.8 dynamic_slice.6
  144.4 0.0 copy-done
  144.4 0.3 fusion.1
  144.6 0.0 copy-start.1
  144.6 26.6 %all-to-all-done.1 = bf16[28,32,512]{2,0,1:T(8,128)(2,1)S(1)} async-done(((bf16[28,32,512]{2,0,1:T(8,128)(2,1)}), bf16[28,32,512]{2,0,1:T(8,128)(2,1)S(1)}, u32[]{:S(2)}, u32[]{:S(2)}) %all-to-all-start.1) | async-done | bytes 917536 | tf_op jit(solution)/shard_map/all_to_all | solution.py:20
  171.2 0.3 fusion
  171.5 17.1 %all-reduce = (f32[512]{0:T(512)S(1)}, f32[512]{0:T(512)S(1)}) all-reduce(f32[512]{0:T(512)S(1)} %fusion.1, f32[512]{0:T(512)S(1)} %fusion), channel_id=1, replica_groups=mesh['section'=8,'fsdp'=32] {'section'}, use_global_device_ids=true, to_apply=%region_1.2 | all-reduce | flops 1024 | bytes 8192 | tf_op jit(solution)/shard_map/psum | solution.py:23
  188.7 1.2 fusion.3
  189.9 0.0 all-gather.6.cloned.1.call-update
  189.9 0.0 all-gather.10.cloned.1.call-start
  189.9 0.8 dynamic_slice.7
  190.7 0.3 convert_bitcast_fusion
  191.0 1.5 reshape.130
  192.5 2.6 multiply_convert_fusion
  195.1 0.0 all-gather.10.cloned.1.call-update
  195.2 0.0 all-gather.8.cloned.1.call-start
  195.2 0.0 copy-done.1
  195.2 0.1 copy.23
  195.3 0.1 copy.18
  195.4 10.0 %all_to_all.48 = bf16[28,8,512]{2,0,1:T(8,128)(2,1)S(1)} all-to-all(bf16[28,8,512]{2,0,1:T(8,128)(2,1)S(1)} %copy.18), channel_id=1, replica_groups=mesh['section'=8,'fsdp'=32] {'section'}, dimensions={1} | all-to-all | bytes 458752 | tf_op jit(solution)/shard_map/all_to_all | solution.py:33
  205.4 0.7 all_to_all.39
  206.1 0.0 all-gather.8.cloned.1.call-update
  206.1 0.0 all-gather.12.cloned.1.call-start
  206.2 1.0 copy.24
  207.2 0.1 copy.22
  207.3 12.0 %all_to_all.49 = bf16[28,8,512]{2,0,1:T(8,128)(2,1)S(1)} all-to-all(bf16[28,8,512]{2,0,1:T(8,128)(2,1)S(1)} %copy.22), channel_id=1, replica_groups=mesh['section'=8,'fsdp'=32] {'section'}, dimensions={1} | all-to-all | bytes 458752 | tf_op jit(solution)/shard_map/all_to_all | solution.py:34
  219.4 0.7 all_to_all.44
  220.1 0.0 all-gather.12.cloned.1.call-update
  220.1 57.8 %all-gather.6.cloned.1.call-done = bf16[512,7168]{1,0:T(8,128)(2,1)} async-done(((bf16[512,896]{1,0:T(8,128)(2,1)}), bf16[512,7168]{1,0:T(8,128)(2,1)}) %all-gather.6.cloned.1.call-update) | async-done | bytes 7340048 | tf_op jit(solution)/shard_map/all_gather | solution.py:37
  278.0 10.4 %copy.16 = bf16[512,7168]{0,1:T(8,128)(2,1)} copy(bf16[512,7168]{1,0:T(8,128)(2,1)} %all-gather.6.cloned.1.call-done) | data formatting | bytes 14680064 | tf_op jit(solution)/shard_map/all_gather | solution.py:37
  288.3 11.6 %reshape.126 = bf16[512,8,32,28]{0,3,2,1:T(8,128)(2,1)} reshape(bf16[512,7168]{0,1:T(8,128)(2,1)} %copy.16) | data formatting | bytes 14680064 | tf_op jit(solution)/shard_map/reshape | solution.py:40
  299.9 8.4 %copy.17 = bf16[512,32,8,28]{0,3,2,1:T(8,128)(2,1)} copy(bf16[512,32,8,28]{0,3,1,2:T(8,128)(2,1)} %bitcast.28) | data formatting | bytes 14680064 | tf_op jit(solution)/shard_map/transpose | solution.py:48
  308.2 11.6 %reshape.127 = bf16[512,7168]{0,1:T(8,128)(2,1)} reshape(bf16[512,32,8,28]{0,3,2,1:T(8,128)(2,1)} %copy.17) | data formatting | bytes 14680064 | tf_op jit(solution)/shard_map/reshape | solution.py:48
  319.8 41.5 %all-gather.10.cloned.1.call-done = bf16[7168,512]{1,0:T(8,128)(2,1)} async-done(((bf16[896,512]{1,0:T(8,128)(2,1)}), bf16[7168,512]{1,0:T(8,128)(2,1)}) %all-gather.10.cloned.1.call-update) | async-done | bytes 7340048 | tf_op jit(solution)/shard_map/all_gather | solution.py:38
  361.3 11.5 %reshape.128 = bf16[8,32,28,512]{3,2,1,0:T(8,128)(2,1)} reshape(bf16[7168,512]{1,0:T(8,128)(2,1)} %all-gather.10.cloned.1.call-done) | data formatting | bytes 14680064 | tf_op jit(solution)/shard_map/reshape | solution.py:41
  372.8 8.5 %copy.21 = bf16[32,8,28,512]{3,2,1,0:T(8,128)(2,1)} copy(bf16[32,8,28,512]{3,2,0,1:T(8,128)(2,1)} %bitcast.29) | data formatting | bytes 14680064 | tf_op jit(solution)/shard_map/transpose | solution.py:50
  381.2 11.6 %reshape.129 = bf16[7168,512]{1,0:T(8,128)(2,1)} reshape(bf16[32,8,28,512]{3,2,1,0:T(8,128)(2,1)} %copy.21) | data formatting | bytes 14680064 | tf_op jit(solution)/shard_map/reshape | solution.py:50
  392.8 43.1 %all-gather.8.cloned.1.call-done = bf16[7168,512]{1,0:T(8,128)(2,1)} async-done(((bf16[224,512]{1,0:T(8,128)(2,1)}), bf16[7168,512]{1,0:T(8,128)(2,1)}) %all-gather.8.cloned.1.call-update) | async-done | bytes 7340048 | tf_op jit(solution)/shard_map/all_gather | solution.py:43
  435.9 8.5 %fusion.5 = f32[512,512]{1,0:T(8,128)S(1)} fusion(bf16[512,7168]{0,1:T(8,128)(2,1)} %reshape.127, bf16[7168,512]{1,0:T(8,128)(2,1)} %all-gather.8.cloned.1.call-done), kind=kOutput, calls=%fused_computation.20 | convolution fusion | flops 3758096384 | bytes 15728640 | tf_op jit(solution)/shard_map/dot_general | solution.py:52
  444.4 65.6 %all-gather.12.cloned.1.call-done = bf16[7168,512]{1,0:T(8,128)(2,1)} async-done(((bf16[224,512]{1,0:T(8,128)(2,1)}), bf16[7168,512]{1,0:T(8,128)(2,1)}) %all-gather.12.cloned.1.call-update) | async-done | bytes 7340048 | tf_op jit(solution)/shard_map/all_gather | solution.py:44
  510.0 10.0 %fusion.4 = bf16[512,512]{1,0:T(8,128)(2,1)} fusion(f32[512,512]{1,0:T(8,128)S(1)} %fusion.5, bf16[7168,512]{1,0:T(8,128)(2,1)} %reshape.129, bf16[7168,512]{1,0:T(8,128)(2,1)} %all-gather.12.cloned.1.call-done), kind=kOutput, calls=%fused_computation.11 | convolution fusion | flops 3758620672 | bytes 16252928 | tf_op jit(solution)/shard_map/dot_general | solution.py:53
  (7 shorter events, 0.1 us)
Async XLA Ops:
  71.6 72.8 %copy-start = (bf16[512,896]{1,0:T(8,128)(2,1)S(1)}, bf16[512,896]{1,0:T(8,128)(2,1)}, u32[]{:S(2)}) copy-start(bf16[512,896]{1,0:T(8,128)(2,1)} %param.7) | copy-start | bytes 2752516
  139.8 31.4 %all-to-all-start.1 = ((bf16[28,32,512]{2,0,1:T(8,128)(2,1)}), bf16[28,32,512]{2,0,1:T(8,128)(2,1)S(1)}, u32[]{:S(2)}, u32[]{:S(2)}) async-start(bf16[28,32,512]{2,0,1:T(8,128)(2,1)} %broadcast_select_fusion), calls=%async_computation.1 | async-start | bytes 2097152 | tf_op jit(solution)/shard_map/all_to_all | solution.py:20
  143.6 134.4 %all-gather.6.cloned.1.call-start = ((), (), s32[]{:S(2)}) async-start(), calls=%async_computation.3 | async-start | bytes 8257536 | tf_op jit(solution)/shard_map/all_gather | solution.py:37
  144.6 50.6 %copy-start.1 = (bf16[28,4096]{1,0:T(8,128)(2,1)S(1)}, bf16[28,4096]{1,0:T(8,128)(2,1)}, u32[]{:S(2)}) copy-start(bf16[28,4096]{1,0:T(8,128)(2,1)} %param.12) | copy-start | bytes 688132
  189.9 171.4 %all-gather.10.cloned.1.call-start = ((), (), s32[]{:S(2)}) async-start(), calls=%async_computation.5 | async-start | bytes 8257536 | tf_op jit(solution)/shard_map/all_gather | solution.py:38
  195.2 240.7 %all-gather.8.cloned.1.call-start = ((), (), s32[]{:S(2)}) async-start(), calls=%async_computation.4 | async-start | bytes 7569408 | tf_op jit(solution)/shard_map/all_gather | solution.py:43
  206.1 303.9 %all-gather.12.cloned.1.call-start = ((), (), s32[]{:S(2)}) async-start(), calls=%async_computation.6 | async-start | bytes 7569408 | tf_op jit(solution)/shard_map/all_gather | solution.py:44
Sparse Core Ops, SparseCore 0:
  190.0 87.8 all-gather.5
  279.7 81.4 all-gather.9
  363.8 72.0 all-gather.7
  438.3 71.6 all-gather.11
where the time goes:
time: 529 us; the launch traced here: 527 us
  waiting for transfers between devices  235 us (44%)
  local copies, waits for them, and re-layouts  161 us (30%)
  blocking collectives  88.1 us (17%)
  matrix products  18.5 us (3%)
  between operations  13.3 us (3%)
  other arithmetic  7.31 us (1%)
    gather x2, local copies, waits for them, and re-layouts, on_device(): looked = jnp.take(table, shifted, axis=1)  67 us
    all_gather x1, waiting for transfers between devices, on_device(): lax.all_gather(embed_panel, 'fsdp', axis=0, tiled=True)  65.6 us
    all_gather x1, waiting for transfers between devices, on_device(): lax.all_gather(hidden_norm, 'section', axis=1, tiled=True)  57.8 us
    all_gather x1, blocking collectives, on_device(): every_id = lax.all_gather(token_ids, 'fsdp', axis=0, tiled=True)  49 us
    all_gather x1, waiting for transfers between devices, on_device(): lax.all_gather(hidden_panel, 'fsdp', axis=0, tiled=True)  43.1 us
    all_gather x1, waiting for transfers between devices, on_device(): lax.all_gather(embed_norm, 'section', axis=0, tiled=True)  41.5 us
    all_to_all x1, waiting for transfers between devices, on_device(): lax.all_to_all(looked, 'fsdp', split_axis=1, concat_axis=0, tiled=True)  26.6 us
    psum x1, blocking collectives, on_device(): lax.psum((jnp.sum(hidden_f * hidden_f, axis=1), jnp.sum(embed_f * embed_f...  17.1 us
  transfers between devices with their start and end apart: 5, of which 5 were waited for; matrix products, arithmetic and copies ran while one was open for 17% of the time, Pallas kernels for 0%

commit v1 on v0

--- a/solution.py
+++ b/solution.py
@@ -17,7 +17,15 @@
     every_id = lax.all_gather(token_ids, "fsdp", axis=0, tiled=True)
     shifted = jnp.roll(every_id, -1)
     looked = jnp.take(table, shifted, axis=1)
-    embed_block = lax.all_to_all(looked, "fsdp", split_axis=1, concat_axis=0, tiled=True)
+    embed_block = jnp.concatenate(
+        lax.all_to_all(
+            jnp.stack(jnp.split(looked, lax.axis_size("fsdp"), axis=1), axis=0),
+            axis_name="fsdp",
+            concat_axis=0,
+            split_axis=0,
+        ),
+        axis=0,
+    )
     hidden_f = hidden.astype(jnp.float32)
     embed_f = embed_block.astype(jnp.float32)
     hidden_sq, embed_sq = lax.psum(

time: 529 us -> 559 us (1.057)
  local copies, waits for them, and re-layouts: 161 us -> 180 us
  other arithmetic: 7.31 us -> 15.4 us
    unnamed x7 -> x40, local copies, waits for them, and re-layouts: 15 us -> 34.5 us
    select_n x2, other arithmetic: 1.88 us -> 11.7 us  [on_device(): looked = jnp.take(table, shifted, axis=1)]
    gather x2 -> x1, local copies, waits for them, and re-layouts: 67 us -> 62.9 us  [on_device(): looked = jnp.take(table, shifted, axis=1)]
  transfers between devices with their start and end apart: 5 -> 5, of which waited for: 5 -> 5; matrix products, arithmetic and copies ran while one was open for 17% -> 15% of each run, Pallas kernels for 0% -> 0%
where the time goes in v1:
time: 559 us; the launch traced here: 557 us
  waiting for transfers between devices  240 us (43%)
  local copies, waits for them, and re-layouts  180 us (32%)
  blocking collectives  86.3 us (15%)
  matrix products  18.5 us (3%)
  other arithmetic  15.4 us (3%)
  between operations  13.3 us (2%)
    all_gather x1, waiting for transfers between devices, on_device(): lax.all_gather(embed_panel, 'fsdp', axis=0, tiled=True)  65.6 us
    gather x1, local copies, waits for them, and re-layouts, on_device(): looked = jnp.take(table, shifted, axis=1)  62.9 us
    all_gather x1, waiting for transfers between devices, on_device(): lax.all_gather(hidden_norm, 'section', axis=1, tiled=True)  62.4 us
    all_gather x1, blocking collectives, on_device(): every_id = lax.all_gather(token_ids, 'fsdp', axis=0, tiled=True)  49 us
    all_gather x1, waiting for transfers between devices, on_device(): lax.all_gather(hidden_panel, 'fsdp', axis=0, tiled=True)  43.1 us
    all_gather x1, waiting for transfers between devices, on_device(): lax.all_gather(embed_norm, 'section', axis=0, tiled=True)  41.8 us
    unnamed x40, local copies, waits for them, and re-layouts  34.5 us
    all_to_all x1, waiting for transfers between devices, on_device(): lax.all_to_all(jnp.stack(jnp.split(looked, lax.axis_size('fsdp'), axis=1)...  26.6 us
  transfers between devices with their start and end apart: 5, of which 5 were waited for; matrix products, arithmetic and copies ran while one was open for 15% of the time, Pallas kernels for 0%

profile of v1, /device:TPU:1, one launch (start us, length us, event | category | flops | bytes accessed | tf_op | source)
XLA Modules:
  0.0 557.1 jit_solution(5061647201506427198)
XLA Ops:
  6.5 49.0 %all-gather = s32[32,1,512]{2,1,0:T(1,128)S(1)} all-gather(s32[1,1,512]{2,1,0:T(1,128)} %bitcast.165), channel_id=1, replica_groups=mesh['section'=8,'fsdp'=32] {'fsdp'}, dimensions={0}, use_global_device_ids=true | all-gather | bytes 67584 | tf_op jit(solution)/shard_map/all_gather | solution.py:17
  55.5 0.5 slice.13
  56.1 13.9 %copy.58 = bf16[28,65536]{0,1:T(8,128)(2,1)} copy(bf16[28,65536]{1,0:T(8,128)(2,1)} %param.9) | data formatting | bytes 7340032 | tf_op args[2]
  70.0 0.7 compare_and_fusion
  70.8 0.8 compare_select_fusion
  71.6 62.9 %gather_fusion = bf16[16384,28]{1,0:T(8,128)(2,1)} fusion(bf16[28,65536]{0,1:T(8,128)(2,1)} %copy.58, s32[16384]{0:T(1024)S(1)} %broadcast_clamp_fusion), kind=kCustom, calls=%fused_computation | custom fusion | bytes 1900544 | tf_op jit(solution)/shard_map/jit(_take)/gather | solution.py:19
  134.5 10.9 %select_bitcast_fusion = bf16[28,16384]{0,1:T(8,128)(2,1)S(1)} fusion(bf16[16384,28]{1,0:T(8,128)(2,1)} %gather_fusion, pred[16384]{0:T(1024)(128)(4,1)S(1)} %compare_and_fusion), kind=kLoop, calls=%fused_computation.1 | loop fusion | flops 458752 | bytes 1851392 | tf_op jit(solution)/shard_map/jit(_take)/select_n | solution.py:19
  145.4 0.7 fusion.35
  146.1 0.7 fusion.34
  146.7 0.6 fusion.33
  147.4 0.7 fusion.32
  148.0 0.7 fusion.31
  148.7 0.7 fusion.30
  149.3 0.7 fusion.29
  150.0 0.7 fusion.28
  150.7 0.7 fusion.27
  151.3 0.7 fusion.26
  152.0 0.7 fusion.25
  152.6 0.7 fusion.24
  153.3 0.7 fusion.23
  154.0 0.7 fusion.22
  154.6 0.6 fusion.21
  155.3 0.7 fusion.20
  155.9 0.7 fusion.19
  156.6 0.7 fusion.18
  157.3 0.7 fusion.17
  157.9 0.7 fusion.16
  158.6 0.7 fusion.15
  159.3 0.7 fusion.14
  159.9 0.7 fusion.13
  160.6 0.7 fusion.12
  161.2 0.7 fusion.11
  161.9 0.7 fusion.10
  162.6 0.6 fusion.9
  163.2 0.6 fusion.8
  163.9 0.7 fusion.7
  164.5 0.7 fusion.6
  165.2 0.6 fusion.5
  165.8 0.6 fusion.4
  166.5 4.7 copy.59
  171.2 3.8 all-to-all-start.1
  175.0 0.8 dynamic_slice.6
  176.0 26.6 %all-to-all-done.1 = bf16[32,28,512]{2,1,0:T(8,128)(2,1)S(1)} async-done(((bf16[32,28,512]{2,1,0:T(8,128)(2,1)}), bf16[32,28,512]{2,1,0:T(8,128)(2,1)S(1)}, u32[]{:S(2)}, u32[]{:S(2)}) %all-to-all-start.1) | async-done | bytes 917536 | tf_op jit(solution)/shard_map/all_to_all | solution.py:21
  202.9 17.1 %all-reduce = (f32[512]{0:T(512)S(1)}, f32[512]{0:T(512)S(1)}) all-reduce(f32[512]{0:T(512)S(1)} %fusion, f32[512]{0:T(512)S(1)} %multiply_reduce_fusion), channel_id=1, replica_groups=mesh['section'=8,'fsdp'=32] {'section'}, use_global_device_ids=true, to_apply=%region_1.2 | all-reduce | flops 1024 | bytes 8192 | tf_op jit(solution)/shard_map/psum | solution.py:31
  220.0 1.2 fusion.2
  221.3 0.8 dynamic_slice.7
  222.3 1.1 multiply_convert_fusion
  223.7 8.5 %all_to_all.43 = bf16[28,8,512]{2,0,1:T(8,128)(2,1)S(1)} all-to-all(bf16[28,8,512]{2,0,1:T(8,128)(2,1)S(1)} %copy.57), channel_id=1, replica_groups=mesh['section'=8,'fsdp'=32] {'section'}, dimensions={1} | all-to-all | bytes 458752 | tf_op jit(solution)/shard_map/all_to_all | solution.py:41
  232.2 0.7 all_to_all.34
  233.2 11.7 %all_to_all.44 = bf16[28,8,512]{2,0,1:T(8,128)(2,1)S(1)} all-to-all(bf16[28,8,512]{2,0,1:T(8,128)(2,1)S(1)} %copy.61), channel_id=1, replica_groups=mesh['section'=8,'fsdp'=32] {'section'}, dimensions={1} | all-to-all | bytes 458752 | tf_op jit(solution)/shard_map/all_to_all | solution.py:42
  244.9 0.7 all_to_all.39
  245.7 62.4 %all-gather.6.cloned.1.call-done = bf16[512,7168]{1,0:T(8,128)(2,1)} async-done(((bf16[512,896]{1,0:T(8,128)(2,1)}), bf16[512,7168]{1,0:T(8,128)(2,1)}) %all-gather.6.cloned.1.call-update) | async-done | bytes 7340048 | tf_op jit(solution)/shard_map/all_gather | solution.py:45
  308.1 10.4 %copy.55 = bf16[512,7168]{0,1:T(8,128)(2,1)} copy(bf16[512,7168]{1,0:T(8,128)(2,1)} %all-gather.6.cloned.1.call-done) | data formatting | bytes 14680064 | tf_op jit(solution)/shard_map/all_gather | solution.py:45
  318.5 11.6 %reshape.118 = bf16[512,8,32,28]{0,3,2,1:T(8,128)(2,1)} reshape(bf16[512,7168]{0,1:T(8,128)(2,1)} %copy.55) | data formatting | bytes 14680064 | tf_op jit(solution)/shard_map/reshape | solution.py:48
  330.1 8.4 %copy.56 = bf16[512,32,8,28]{0,3,2,1:T(8,128)(2,1)} copy(bf16[512,32,8,28]{0,3,1,2:T(8,128)(2,1)} %bitcast.153) | data formatting | bytes 14680064 | tf_op jit(solution)/shard_map/transpose | solution.py:56
  338.5 11.6 %reshape.119 = bf16[512,7168]{0,1:T(8,128)(2,1)} reshape(bf16[512,32,8,28]{0,3,2,1:T(8,128)(2,1)} %copy.56) | data formatting | bytes 14680064 | tf_op jit(solution)/shard_map/reshape | solution.py:56
  350.0 41.8 %all-gather.10.cloned.1.call-done = bf16[7168,512]{1,0:T(8,128)(2,1)} async-done(((bf16[896,512]{1,0:T(8,128)(2,1)}), bf16[7168,512]{1,0:T(8,128)(2,1)}) %all-gather.10.cloned.1.call-update) | async-done | bytes 7340048 | tf_op jit(solution)/shard_map/all_gather | solution.py:46
  391.8 11.5 %reshape.120 = bf16[8,32,28,512]{3,2,1,0:T(8,128)(2,1)} reshape(bf16[7168,512]{1,0:T(8,128)(2,1)} %all-gather.10.cloned.1.call-done) | data formatting | bytes 14680064 | tf_op jit(solution)/shard_map/reshape | solution.py:49
  403.3 8.4 %copy.60 = bf16[32,8,28,512]{3,2,1,0:T(8,128)(2,1)} copy(bf16[32,8,28,512]{3,2,0,1:T(8,128)(2,1)} %bitcast.154) | data formatting | bytes 14680064 | tf_op jit(solution)/shard_map/transpose | solution.py:58
  411.8 11.6 %reshape.121 = bf16[7168,512]{1,0:T(8,128)(2,1)} reshape(bf16[32,8,28,512]{3,2,1,0:T(8,128)(2,1)} %copy.60) | data formatting | bytes 14680064 | tf_op jit(solution)/shard_map/reshape | solution.py:58
  423.3 43.1 %all-gather.8.cloned.1.call-done = bf16[7168,512]{1,0:T(8,128)(2,1)} async-done(((bf16[224,512]{1,0:T(8,128)(2,1)}), bf16[7168,512]{1,0:T(8,128)(2,1)}) %all-gather.8.cloned.1.call-update) | async-done | bytes 7340048 | tf_op jit(solution)/shard_map/all_gather | solution.py:51
  466.4 8.5 %fusion.36 = f32[512,512]{1,0:T(8,128)S(1)} fusion(bf16[512,7168]{0,1:T(8,128)(2,1)} %reshape.119, bf16[7168,512]{1,0:T(8,128)(2,1)} %all-gather.8.cloned.1.call-done), kind=kOutput, calls=%fused_computation.81 | convolution fusion | flops 3758096384 | bytes 15728640 | tf_op jit(solution)/shard_map/dot_general | solution.py:60
  474.9 65.6 %all-gather.12.cloned.1.call-done = bf16[7168,512]{1,0:T(8,128)(2,1)} async-done(((bf16[224,512]{1,0:T(8,128)(2,1)}), bf16[7168,512]{1,0:T(8,128)(2,1)}) %all-gather.12.cloned.1.call-update) | async-done | bytes 7340048 | tf_op jit(solution)/shard_map/all_gather | solution.py:52
  540.5 10.0 %fusion.3 = bf16[512,512]{1,0:T(8,128)(2,1)} fusion(f32[512,512]{1,0:T(8,128)S(1)} %fusion.36, bf16[7168,512]{1,0:T(8,128)(2,1)} %reshape.121, bf16[7168,512]{1,0:T(8,128)(2,1)} %all-gather.12.cloned.1.call-done), kind=kOutput, calls=%fused_computation.10 | convolution fusion | flops 3758620672 | bytes 16252928 | tf_op jit(solution)/shard_map/dot_general | solution.py:61
  (27 shorter events, 1.4 us)
Async XLA Ops:
  163.9 11.9 %copy-start = (bf16[512,896]{1,0:T(8,128)(2,1)S(1)}, bf16[512,896]{1,0:T(8,128)(2,1)}, u32[]{:S(2)}) copy-start(bf16[512,896]{1,0:T(8,128)(2,1)} %param.7) | copy-start | bytes 2752516
  171.2 31.4 %all-to-all-start.1 = ((bf16[32,28,512]{2,1,0:T(8,128)(2,1)}), bf16[32,28,512]{2,1,0:T(8,128)(2,1)S(1)}, u32[]{:S(2)}, u32[]{:S(2)}) async-start(bf16[32,28,512]{2,1,0:T(8,128)(2,1)} %copy.59), calls=%async_computation.1 | async-start | bytes 2097152 | tf_op jit(solution)/shard_map/all_to_all | solution.py:21
  174.9 133.2 %all-gather.6.cloned.1.call-start = ((), (), s32[]{:S(2)}) async-start(), calls=%async_computation.3 | async-start | bytes 8257536 | tf_op jit(solution)/shard_map/all_gather | solution.py:45
  221.2 2.3 copy-start.1
  221.3 170.5 %all-gather.10.cloned.1.call-start = ((), (), s32[]{:S(2)}) async-start(), calls=%async_computation.5 | async-start | bytes 8257536 | tf_op jit(solution)/shard_map/all_gather | solution.py:46
  222.1 10.9 %copy-start.2 = (bf16[28,4096]{1,0:T(8,128)(2,1)S(1)}, bf16[28,4096]{1,0:T(8,128)(2,1)}, u32[]{:S(2)}) copy-start(bf16[28,4096]{1,0:T(8,128)(2,1)} %param.13) | copy-start | bytes 688132
  223.5 243.0 %all-gather.8.cloned.1.call-start = ((), (), s32[]{:S(2)}) async-start(), calls=%async_computation.4 | async-start | bytes 7569408 | tf_op jit(solution)/shard_map/all_gather | solution.py:51
  233.0 307.6 %all-gather.12.cloned.1.call-start = ((), (), s32[]{:S(2)}) async-start(), calls=%async_computation.6 | async-start | bytes 7569408 | tf_op jit(solution)/shard_map/all_gather | solution.py:52
Sparse Core Ops, SparseCore 0:
  221.4 86.6 all-gather.5
  309.9 81.8 all-gather.9
  394.3 72.0 all-gather.7
  468.8 71.6 all-gather.11
